TPU v7x, 32 devices: a whole 2x2x4 slice. The times are simulated.
32 devices in a mesh: guide: 2 (over core), blk: 4 (over z), batch: 4 (over y, x).
Axes of the slice: x: 2, y: 2, z: 4, core: 2. Of those that a mesh axis runs over, the one named last changes fastest.
Arguments:
- hidden: bfloat16 [2, 64, 1536], P('guide', 'batch'), may hold values from -6 to 6
- w_qkv: bfloat16 [1536, 2560], P('blk'), may hold values from -0.15625 to 0.15625
- key_cache: bfloat16 [2, 64, 64, 512], P('guide', 'batch', 'blk'), may hold values from -700 to 700
- value_cache: bfloat16 [2, 64, 64, 512], P('guide', 'batch', 'blk'), may hold values from -6 to 6
- lengths: int32 [2, 64], P('guide', 'batch'), may hold values from 8 to 64, as said below
- w_out: bfloat16 [1536, 1536], P('blk'), may hold values from -0.15625 to 0.15625
- router: bfloat16 [1536, 16], replicated, may hold values from -0.15625 to 0.15625
- routes: int32 [2, 64, 2], P('guide', 'batch'), may hold values from 0 to 15, all different within a row
- w_gate: bfloat16 [1536, 16384], P(None, 'blk'), may hold values from -0.15625 to 0.15625
- w_up: bfloat16 [1536, 16384], P(None, 'blk'), may hold values from -0.15625 to 0.15625
- w_down: bfloat16 [16384, 1536], P('blk'), may hold values from -0.125 to 0.125
- w_vocab: bfloat16 [1536, 65536], P(None, ('blk', 'batch')), may hold values from -0.15625 to 0.15625
- group_ids: int32 [64], replicated, may hold values from 0 to 7, never falling along the last dimension, each value on 1 to 16 neighbouring positions
- weight_index: int32 [8], replicated, may hold values from 0 to 7
- guidance_levels: float32 [8], replicated, may hold values from 1 to 5
Outputs:
- logits: float32 [64, 65536], P('guide', ('blk', 'batch'))
- new_keys: bfloat16 [2, 64, 512], P('guide', 'batch')
- new_values: bfloat16 [2, 64, 512], P('guide', 'batch')
Inputs may be any that keep to these rules, and one draw needn't show every extreme that they name: `lengths`: every stream and index of batch has a request whose cache is full.
All inputs are finite; a program needn't handle non-finite values.
Results may differ from a plain program's by a relative error of at most 0.008.
Values may be sent and summed in bfloat16 or wider, within the bound.
A program may use at most 128 MiB of HBM per device.

v0:
```python
import jax
import jax.numpy as jnp
from jax import lax
from jax.sharding import PartitionSpec as P

HEADS = 24
KV_HEADS = 8
HEAD_DIM = 64
EXPERTS = 16
EXPERT_UNITS = 1024


EPS = 1e-05


def from_partner(value, axis, bit):
    mask = 2**bit
    pairs = [(source, source ^ mask) for source in range(lax.axis_size(axis))]
    return lax.ppermute(value, axis, pairs)


def rms(values):
    return values * lax.rsqrt(jnp.mean(values * values, axis=-1, keepdims=True) + EPS)


def local(
    hidden,
    w_qkv,
    key_cache,
    value_cache,
    lengths,
    w_out,
    router,
    routes,
    w_gate,
    w_up,
    w_down,
    w_vocab,
    group_ids,
    weight_index,
    guidance_levels,
):
    width_q = HEADS * HEAD_DIM
    width_k = KV_HEADS * HEAD_DIM
    group = HEADS // KV_HEADS
    position_block = lax.axis_index("blk")
    count = hidden.shape[1]
    x = hidden[0].astype(jnp.float32)
    normed = rms(x).astype(jnp.bfloat16)
    feat_rows = w_qkv.shape[0]
    normed_part = lax.dynamic_slice_in_dim(normed, position_block * feat_rows, feat_rows, 1)
    partial_qkv = jnp.dot(normed_part, w_qkv, preferred_element_type=jnp.float32)
    qkv = lax.psum(partial_qkv, "blk").astype(jnp.bfloat16)
    query = qkv[:, :width_q]
    new_key = qkv[:, width_q : width_q + width_k]
    new_value = qkv[:, width_q + width_k :]
    span = key_cache.shape[2]
    query_heads = query.reshape(count, KV_HEADS, group, HEAD_DIM)
    keys_here = key_cache[0].reshape(count, span, KV_HEADS, HEAD_DIM)
    values_here = value_cache[0].reshape(count, span, KV_HEADS, HEAD_DIM)
    scale = HEAD_DIM ** (-0.5)
    scores = (
        jnp.einsum("rkgd,rckd->rkgc", query_heads, keys_here, preferred_element_type=jnp.float32)
        * scale
    )
    own = (
        jnp.einsum(
            "rkgd,rkd->rkg",
            query_heads,
            new_key.reshape(count, KV_HEADS, HEAD_DIM),
            preferred_element_type=jnp.float32,
        )
        * scale
    )
    positions = position_block * span + jnp.arange(span)
    valid = (positions[None, :] < lengths[0][:, None])[:, None, None, :]
    local_top = jnp.max(jnp.where(valid, scores, -1e30), axis=-1)
    top = lax.pmax(jnp.maximum(local_top, own), "blk")
    probs = jnp.exp(jnp.where(valid, scores - top[..., None], -1e30))
    partial_total = jnp.sum(probs, axis=-1)
    acc = jnp.einsum(
        "rkgc,rckd->rkgd",
        probs.astype(jnp.bfloat16),
        values_here,
        preferred_element_type=jnp.float32,
    ).reshape(count, width_q)
    own_prob = jnp.exp(own - top)
    own_rounded = lax.optimization_barrier(own_prob.astype(jnp.bfloat16)).astype(jnp.float32)
    own_term = (
        own_rounded[..., None] * new_value.astype(jnp.float32).reshape(count, KV_HEADS, 1, HEAD_DIM)
    ).reshape(count, width_q)
    out_rows = w_out.shape[0]
    acc_sum, total_sum = lax.psum((acc, partial_total), "blk")
    totals = jnp.repeat((total_sum + own_prob).reshape(count, HEADS), HEAD_DIM, axis=1)
    attn = ((acc_sum + own_term) / totals).astype(jnp.bfloat16)
    attn_cols = lax.dynamic_slice_in_dim(attn, position_block * out_rows, out_rows, 1)
    mixed = x + lax.psum(jnp.dot(attn_cols, w_out, preferred_element_type=jnp.float32), "blk")
    expert_in = rms(mixed).astype(jnp.bfloat16)
    choice_logits = jnp.dot(expert_in, router, preferred_element_type=jnp.float32)
    picks = (routes[0][:, :, None] == jnp.arange(EXPERTS)[None, None, :]).astype(jnp.float32)
    chosen = jnp.sum(picks * choice_logits[:, None, :], axis=-1)
    first = jax.nn.sigmoid(chosen[:, 0] - chosen[:, 1])
    shares = jnp.stack([first, 1.0 - first], axis=1)
    per_expert = jnp.sum(picks * shares[:, :, None], axis=1)
    local_units = w_gate.shape[1]
    owner = (position_block * local_units + jnp.arange(local_units)) // EXPERT_UNITS
    member = (owner[None, :] == jnp.arange(EXPERTS)[:, None]).astype(jnp.float32)
    unit_weight = jnp.sum(per_expert[:, :, None] * member[None, :, :], axis=1)
    gate = jnp.dot(expert_in, w_gate, preferred_element_type=jnp.float32)
    upper = jnp.dot(expert_in, w_up, preferred_element_type=jnp.float32)
    act = (jax.nn.silu(gate) * upper * unit_weight).astype(jnp.bfloat16)
    expert_out = lax.psum(jnp.dot(act, w_down, preferred_element_type=jnp.float32), "blk")
    final_in = rms(mixed + expert_out).astype(jnp.bfloat16)
    stream_logits = jnp.dot(
        lax.all_gather(final_in, "batch", axis=0, tiled=True),
        w_vocab,
        preferred_element_type=jnp.float32,
    ).astype(jnp.bfloat16)
    stream_index = lax.axis_index("guide")
    half_rows = stream_logits.shape[0] // 2
    kept_rows = lax.dynamic_slice_in_dim(stream_logits, stream_index * half_rows, half_rows, 0)
    sent_rows = lax.dynamic_slice_in_dim(
        stream_logits, (1 - stream_index) * half_rows, half_rows, 0
    )
    partner = from_partner(sent_rows, "guide", 0)
    is_first = stream_index == 0
    cond = jnp.where(is_first, kept_rows, partner).astype(jnp.float32)
    uncond = jnp.where(is_first, partner, kept_rows).astype(jnp.float32)
    group_count = weight_index.shape[0]
    level_count = guidance_levels.shape[0]
    in_group = (group_ids[:, None] == jnp.arange(group_count)[None, :]).astype(jnp.float32)
    level_pick = (weight_index[:, None] == jnp.arange(level_count)[None, :]).astype(jnp.float32)
    group_weight = jnp.sum(level_pick * guidance_levels[None, :], axis=1)
    request_weight = jnp.sum(in_group * group_weight[None, :], axis=1)
    weight_rows = lax.dynamic_slice_in_dim(request_weight, stream_index * half_rows, half_rows, 0)
    logits = uncond + weight_rows[:, None] * (cond - uncond)
    return (logits, new_key[None], new_value[None])


def solution(mesh):
    placed = (
        P("guide", "batch", None),
        P("blk", None),
        P("guide", "batch", "blk", None),
        P("guide", "batch", "blk", None),
        P("guide", "batch"),
        P("blk", None),
        P(),
        P("guide", "batch", None),
        P(None, "blk"),
        P(None, "blk"),
        P("blk", None),
        P(None, ("blk", "batch")),
        P(),
        P(),
        P(),
    )
    return jax.shard_map(
        local,
        mesh=mesh,
        in_specs=placed,
        out_specs=(
            P("guide", ("blk", "batch")),
            P("guide", "batch", None),
            P("guide", "batch", None),
        ),
        check_vma=False,
    )
```

profile of v0, /device:TPU:0, one launch (start us, length us, event | category | flops | bytes accessed | tf_op | source)
XLA Modules:
  0.0 209.2 jit_solution(3321609921827451919)
XLA Ops:
  7.2 0.0 copy-start
  7.2 0.0 copy-start.1
  7.2 0.0 copy-start.3
  7.2 0.0 copy-start.4
  7.2 0.0 all-reduce.5.cloned.1.call-start
  7.3 0.9 bitcast_convert_fusion
  8.2 0.9 multiply_reduce_fusion.3
  9.1 0.0 copy-done
  9.1 0.4 fusion.28
  9.5 23.6 %all-reduce.10 = bf16[16,2560]{1,0:T(8,128)(2,1)S(1)} all-reduce(f32[16,2560]{1,0:T(8,128)S(1)} %fusion.28), channel_id=1, replica_groups=mesh['guide'=2,'blk'=4,'batch'=4] {'blk'}, use_global_device_ids=true, to_apply=%region_1.0 | all-reduce | flops 40960 | bytes 245760 | tf_op jit(solution)/shard_map/psum | solution.py:53
  33.1 0.6 slice_bitcast_fusion
  33.8 0.1 reshape.144
  33.9 0.2 reshape.134
  34.0 1.3 reshape_squeeze.6
  35.3 0.3 fusion.37
  35.6 0.7 broadcast_compare_fusion
  36.3 0.5 select_reduce_fusion
  36.8 16.3 %pmax.7 = f32[16,8,3]{2,1,0:T(8,128)S(1)} all-reduce(f32[16,8,3]{2,1,0:T(8,128)S(1)} %multiply_maximum_fusion), channel_id=1, replica_groups=mesh['guide'=2,'blk'=4,'batch'=4] {'blk'}, use_global_device_ids=true, to_apply=%region_3.4 | all-reduce | flops 384 | bytes 3072 | tf_op jit(solution)/shard_map/pmax | solution.py:78
  53.2 1.3 reshape_squeeze.7
  54.4 0.3 fusion.4
  54.8 0.8 reshape.136
  55.6 0.0 all-reduce.5.cloned.1.call-update
  55.6 0.0 all-reduce.7.cloned.1.call-start
  55.7 0.4 fusion.13
  56.1 18.8 %psum.37 = f32[16,8,3]{2,1,0:T(8,128)S(1)} all-reduce(f32[16,8,3]{2,1,0:T(8,128)S(1)} %fusion.13), channel_id=1, replica_groups=mesh['guide'=2,'blk'=4,'batch'=4] {'blk'}, use_global_device_ids=true, to_apply=%region_6.7 | all-reduce | flops 384 | bytes 3072 | tf_op jit(solution)/shard_map/psum | solution.py:93
  75.0 0.1 reshape.140
  75.1 0.2 broadcast_multiply_fusion
  75.3 0.2 mul.161
  75.5 0.1 reshape.145
  75.6 0.1 broadcast_in_dim.24
  75.7 0.1 reshape.138
  75.8 13.8 %all-reduce.5.cloned.1.call-done = f32[16,1536]{1,0:T(8,128)} async-done(((f32[16,1536]{1,0:T(8,128)}), f32[16,1536]{1,0:T(8,128)}) %all-reduce.5.cloned.1.call-update) | async-done | bytes 98320 | tf_op jit(solution)/shard_map/psum | solution.py:93
  89.6 2.2 %fusion.30 = f32[16,1536]{1,0:T(8,128)} fusion(bf16[384,1536]{1,0:T(8,128)(2,1)} %param.20, f32[16,1536]{1,0:T(8,128)S(1)} %reshape.138, s32[]{:T(128)S(6)} %select_n.40, f32[16,1536]{1,0:T(8,128)S(1)} %mul.161, f32[16,1536]{1,0:T(8,128)} %all-reduce.5.cloned.1.call-done), kind=kOutput, calls=%fused_computation.61 | convolution fusion | flops 18892800 | bytes 1351684 | tf_op jit(solution)/shard_map/dot_general | solution.py:97
  91.8 0.0 all-reduce.7.cloned.1.call-update
  91.8 0.0 all-reduce.9.cloned.1.call-start
  91.9 34.7 %all-reduce.7.cloned.1.call-done = f32[16,1536]{1,0:T(8,128)} async-done(((f32[16,1536]{1,0:T(8,128)}), f32[16,1536]{1,0:T(8,128)}) %all-reduce.7.cloned.1.call-update) | async-done | bytes 98320 | tf_op jit(solution)/shard_map/psum | solution.py:97
  126.6 0.0 copy-done.1
  126.6 1.0 multiply_reduce_fusion.2
  127.6 1.0 multiply_convert_fusion.1
  128.6 0.0 copy-done.3
  128.6 0.1 fusion.39
  128.7 0.0 copy-done.4
  128.7 0.2 select_reduce_fusion.2
  128.9 0.1 select_reduce_fusion.1
  129.0 6.3 %fusion.38 = f32[16,4096]{1,0:T(8,128)S(1)} fusion(bf16[16,1536]{1,0:T(8,128)(2,1)S(1)} %multiply_convert_fusion.1, bf16[1536,4096]{1,0:T(8,128)(2,1)} %param.23), kind=kOutput, calls=%fused_computation.82 | convolution fusion | flops 201326592 | bytes 12894208 | tf_op jit(solution)/shard_map/dot_general | solution.py:109
  135.3 0.8 multiply_reduce_fusion
  136.2 0.0 copy-start.2
  136.2 12.2 %fusion.2 = f32[16,1536]{1,0:T(8,128)} fusion(bf16[4096,1536]{1,0:T(8,128)(2,1)} %param.25, f32[16,4096]{1,0:T(8,128)S(1)} %multiply_reduce_fusion, bf16[16,1536]{1,0:T(8,128)(2,1)S(1)} %multiply_convert_fusion.1, bf16[1536,4096]{1,0:T(8,128)(2,1)} %param.24, f32[16,4096]{1,0:T(8,128)S(1)} %fusion.38), kind=kOutput, calls=%fused_computation.8 | convolution fusion | flops 403111936 | bytes 25837568 | tf_op jit(solution)/shard_map/dot_general | solution.py:112
  148.4 0.0 all-reduce.9.cloned.1.call-update
  148.4 34.1 %all-reduce.9.cloned.1.call-done = f32[16,1536]{1,0:T(8,128)} async-done(((f32[16,1536]{1,0:T(8,128)}), f32[16,1536]{1,0:T(8,128)}) %all-reduce.9.cloned.1.call-update) | async-done | bytes 98320 | tf_op jit(solution)/shard_map/psum | solution.py:112
  182.5 0.0 copy-done.2
  182.5 1.0 multiply_reduce_fusion.1
  183.6 1.0 multiply_convert_fusion
  184.6 8.7 %all_gather.3 = bf16[64,1536]{1,0:T(8,128)(2,1)S(1)} all-gather(bf16[16,1536]{1,0:T(8,128)(2,1)S(1)} %multiply_convert_fusion), channel_id=1, replica_groups=mesh['guide'=2,'blk'=4,'batch'=4] {'batch'}, dimensions={0}, use_global_device_ids=true | all-gather | bytes 245760 | tf_op jit(solution)/shard_map/all_gather | solution.py:115
  193.2 6.9 %convolution_convert_fusion = bf16[64,4096]{1,0:T(8,128)(2,1)S(1)} fusion(bf16[64,1536]{1,0:T(8,128)(2,1)S(1)} %all_gather.3, bf16[1536,4096]{1,0:T(8,128)(2,1)} %param.26), kind=kOutput, calls=%fused_computation | convolution fusion | flops 805568512 | bytes 13303808 | tf_op jit(solution)/shard_map/dot_general | solution.py:114
  200.1 0.1 collective-permute-start
  200.2 0.0 copy-done.5
  200.2 0.0 copy-done.6
  200.2 0.2 select_reduce_fusion.4
  200.4 0.0 copy-done.7
  200.4 0.1 select_reduce_fusion.3
  200.5 0.1 dynamic_slice.19
  200.6 1.1 collective-permute-done
  201.7 0.9 convert_add_fusion
  (16 shorter events, 0.2 us)
Async XLA Ops:
  7.2 2.0 copy-start
  7.2 119.4 %copy-start.1 = (bf16[1,16,1536]{2,1,0:T(8,128)(2,1)S(1)}, bf16[1,16,1536]{2,1,0:T(8,128)(2,1)}, u32[]{:S(2)}) copy-start(bf16[1,16,1536]{2,1,0:T(8,128)(2,1)} %param.15) | copy-start | bytes 147460
  7.2 121.4 %copy-start.3 = (bf16[1536,16]{0,1:T(8,128)(2,1)S(1)}, bf16[1536,16]{0,1:T(8,128)(2,1)}, u32[]{:S(2)}) copy-start(bf16[1536,16]{0,1:T(8,128)(2,1)} %param.21) | copy-start | bytes 147460
  7.2 121.5 %copy-start.4 = (s32[1,16,2]{1,2,0:T(2,128)S(1)}, s32[1,16,2]{1,2,0:T(2,128)}, u32[]{:S(2)}) copy-start(s32[1,16,2]{1,2,0:T(2,128)} %param.22) | copy-start | bytes 388
  7.2 82.4 %all-reduce.5.cloned.1.call-start = ((), (), s32[]{:S(2)}) async-start(), calls=%async_computation | async-start | bytes 196608 | tf_op jit(solution)/shard_map/psum | solution.py:93
  55.6 71.0 %all-reduce.7.cloned.1.call-start = ((), (), s32[]{:S(2)}) async-start(), calls=%async_computation.1 | async-start | bytes 196608 | tf_op jit(solution)/shard_map/psum | solution.py:97
  91.8 90.7 %all-reduce.9.cloned.1.call-start = ((), (), s32[]{:S(2)}) async-start(), calls=%async_computation.2 | async-start | bytes 196608 | tf_op jit(solution)/shard_map/psum | solution.py:112
  136.2 46.4 %copy-start.2 = (f32[16,1536]{1,0:T(8,128)S(1)}, f32[16,1536]{1,0:T(8,128)}, u32[]{:S(2)}) copy-start(f32[16,1536]{1,0:T(8,128)} %all-reduce.7.cloned.1.call-done) | copy-start | bytes 294916
  148.4 51.8 %copy-start.5 = (f32[8]{0:T(128)S(1)}, f32[8]{0:T(128)}, u32[]{:S(2)}) copy-start(f32[8]{0:T(128)} %param.29) | copy-start | bytes 100
  148.4 51.8 %copy-start.6 = (s32[8]{0:T(128)S(1)}, s32[8]{0:T(128)}, u32[]{:S(2)}) copy-start(s32[8]{0:T(128)} %param.28) | copy-start | bytes 100
  148.4 52.0 %copy-start.7 = (s32[64]{0:T(128)S(1)}, s32[64]{0:T(128)}, u32[]{:S(2)}) copy-start(s32[64]{0:T(128)} %param.27) | copy-start | bytes 772
  200.1 1.6 collective-permute-start
Sparse Core Ops, SparseCore 0:
  55.8 33.8 all-reduce.4
  92.6 33.9 all-reduce.6
  148.5 33.9 all-reduce.8
where the time goes:
time: 210 us; the launch traced here: 209 us
  waiting for transfers between devices  83.8 us (40%)
  blocking collectives  67.4 us (32%)
  matrix products  29.2 us (14%)
  between operations  14 us (7%)
  other arithmetic  10.2 us (5%)
  local copies, waits for them, and re-layouts  4.36 us (2%)
    psum x1, waiting for transfers between devices, local(): lax.psum(jnp.dot(attn_cols, w_out, preferred_element_type=jnp.float32), '...  34.7 us
    psum x1, waiting for transfers between devices, local(): lax.psum(jnp.dot(act, w_down, preferred_element_type=jnp.float32), 'blk')  34.1 us
    psum x1, blocking collectives, local(): qkv = lax.psum(partial_qkv, 'blk').astype(jnp.bfloat16)  23.6 us
    psum x1, blocking collectives, local(): acc_sum, total_sum = lax.psum((acc, partial_total), 'blk')  18.8 us
    pmax x1, blocking collectives, local(): top = lax.pmax(jnp.maximum(local_top, own), 'blk')  16.3 us
    psum x1, waiting for transfers between devices, local(): acc_sum, total_sum = lax.psum((acc, partial_total), 'blk')  13.8 us
    dot_general x1, matrix products, local(): jnp.dot(act, w_down, preferred_element_type=jnp.float32)  12.2 us
    all_gather x1, blocking collectives, local(): lax.all_gather(final_in, 'batch', axis=0, tiled=True)  8.65 us
  transfers between devices with their start and end apart: 4, of which 4 were waited for; matrix products, arithmetic and copies ran while one was open for 1% of the time, Pallas kernels for 0%

commit v1 on v0

--- a/solution.py
+++ b/solution.py
@@ -1,6 +1,10 @@
+import functools
+
 import jax
 import jax.numpy as jnp
 from jax import lax
+from jax.experimental import pallas as pl
+from jax.experimental.pallas import tpu as pltpu
 from jax.sharding import PartitionSpec as P
 
 HEADS = 24
@@ -137,7 +141,539 @@
     return (logits, new_key[None], new_value[None])
 
 
+TILE = 512
+LANES = 128
+MESH = pl.DeviceIdType.MESH
+F32 = jnp.float32
+BF16 = jnp.bfloat16
+HIGH = lax.Precision.HIGHEST
+PHASES = 8
+QKV_SUM, QKV_ALL, ATT_SUM, ATT_STAT, OUT_SUM, MIX_ALL, EXP_SUM, FIN_ALL = range(PHASES)
+
+
+def iota(shape, dim):
+    return lax.broadcasted_iota(jnp.int32, shape, dim)
+
+
+def step_kernel(
+    n,
+    nb,
+    hidden,
+    lengths,
+    router,
+    routes,
+    group_ids,
+    weight_index,
+    levels,
+    w_qkv,
+    key_cache,
+    value_cache,
+    w_out,
+    w_gate,
+    w_up,
+    w_down,
+    w_vocab,
+    logits_o,
+    keys_o,
+    values_o,
+    qkv_v,
+    key_v,
+    value_v,
+    out_v,
+    gate_v,
+    up_v,
+    down_v,
+    vocab_v,
+    qkv_part,
+    qkv_sum,
+    qkv_all,
+    att_part,
+    att_sum,
+    att_stat,
+    out_part,
+    out_sum,
+    mix_all,
+    exp_part,
+    exp_sum,
+    fin_all,
+    final_own,
+    final_all,
+    load_sem,
+    tile_sem,
+    send_sem,
+    recv_sem,
+    fin_send,
+    fin_recv,
+):
+    g = lax.axis_index("guide")
+    b = lax.axis_index("blk")
+    t = lax.axis_index("batch")
+    half = nb // 2
+    count, width = hidden.shape[1:]
+    span = key_cache.shape[2]
+    cols = width // n
+    kv_width = key_cache.shape[3]
+    group = HEADS // KV_HEADS
+    tiles = gate_v.shape[0]
+    vocab_tiles = vocab_v.shape[0]
+    my_cols = pl.ds(pl.multiple_of(b * cols, LANES), cols)
+
+    loads = [
+        pltpu.make_async_copy(w_qkv, qkv_v, load_sem.at[0]),
+        pltpu.make_async_copy(key_cache.at[0], key_v, load_sem.at[1]),
+        pltpu.make_async_copy(value_cache.at[0], value_v, load_sem.at[2]),
+        pltpu.make_async_copy(w_out, out_v, load_sem.at[3]),
+    ]
+    for load in loads:
+        load.start()
+
+    barrier = pltpu.get_barrier_semaphore()
+    for k in range(1, n):
+        pl.semaphore_signal(
+            barrier, inc=1, device_id={"blk": lax.rem(b + k, n)}, device_id_type=MESH
+        )
+    for k in range(1, 2 * nb):
+        other = lax.rem(g * nb + t + k, 2 * nb)
+        pl.semaphore_signal(
+            barrier,
+            inc=1,
+            device_id={"guide": other // nb, "batch": lax.rem(other, nb)},
+            device_id_type=MESH,
+        )
+
+    def tile_cols(i):
+        return pl.ds(pl.multiple_of(i * TILE, TILE), TILE)
+
+    def gate_load(i):
+        return pltpu.make_async_copy(w_gate.at[:, tile_cols(i)], gate_v.at[i], tile_sem.at[0, i])
+
+    def up_load(i):
+        return pltpu.make_async_copy(w_up.at[:, tile_cols(i)], up_v.at[i], tile_sem.at[1, i])
+
+    def down_load(i):
+        return pltpu.make_async_copy(w_down.at[tile_cols(i), :], down_v.at[i], tile_sem.at[2, i])
+
+    def vocab_load(i):
+        return pltpu.make_async_copy(w_vocab.at[:, tile_cols(i)], vocab_v.at[i], tile_sem.at[3, i])
+
+    def send(phase, source, landing):
+        for k in range(1, n):
+            peer = lax.rem(b + k, n)
+            pltpu.make_async_remote_copy(
+                src_ref=source(peer),
+                dst_ref=landing.at[b],
+                send_sem=send_sem.at[phase, k - 1],
+                recv_sem=recv_sem.at[phase, b],
+                device_id={"blk": peer},
+                device_id_type=MESH,
+            ).start()
+
+    def arrive(phase, landing):
+        for k in range(1, n):
+            peer = lax.rem(b + k, n)
+            pltpu.make_async_remote_copy(
+                src_ref=landing.at[peer],
+                dst_ref=landing.at[peer],
+                send_sem=send_sem.at[phase, k - 1],
+                recv_sem=recv_sem.at[phase, peer],
+                device_id={"blk": peer},
+                device_id_type=MESH,
+            ).wait_recv()
+
+    def drain(phase, landing):
+        for k in range(1, n):
+            peer = lax.rem(b + k, n)
+            pltpu.make_async_remote_copy(
+                src_ref=landing.at[b],
+                dst_ref=landing.at[b],
+                send_sem=send_sem.at[phase, k - 1],
+                recv_sem=recv_sem.at[phase, b],
+                device_id={"blk": peer},
+                device_id_type=MESH,
+            ).wait_send()
+
+    def summed(landing):
+        total = landing[0].astype(F32)
+        for j in range(1, n):
+            total = total + landing[j].astype(F32)
+        return total
+
+    def joined(landing):
+        return jnp.concatenate([landing[j] for j in range(n)], axis=1)
+
+    def inverse_rms(values):
+        return lax.rsqrt(jnp.mean(values * values, axis=-1, keepdims=True) + EPS)
+
+    inverse = inverse_rms(hidden[0].astype(F32))
+    normed = (hidden[0, :, my_cols].astype(F32) * inverse).astype(BF16)
+    loads[0].wait()
+
+    def start_expert(i, carry):
+        gate_load(i).start()
+        up_load(i).start()
+        down_load(i).start()
+        return carry
+
+    def start_vocab(i, carry):
+        vocab_load(i).start()
+        return carry
+
+    for j in range(n):
+        starts = (
+            (0, cols, j * cols),
+            (cols, LANES, width + j * LANES),
+            (cols + LANES, LANES, width + kv_width + j * LANES),
+        )
+        for at, size, begin in starts:
+            qkv_part[j, :, at : at + size] = jnp.dot(
+                normed, qkv_v[:, begin : begin + size], preferred_element_type=F32
+            )
+    qkv_sum[b] = qkv_part[b]
+    pl.semaphore_wait(barrier, n - 1 + 2 * nb - 1)
+    send(QKV_SUM, lambda peer: qkv_part.at[peer], qkv_sum)
+    lax.fori_loop(0, tiles, start_expert, 0)
+    lax.fori_loop(0, vocab_tiles, start_vocab, 0)
+
+    kept = final_all.shape[0] // 2 * count
+    row = iota((kept, 1), 0)
+
+    def pick_weight(i, column):
+        level = levels[weight_index[group_ids[g * kept + i]]]
+        return jnp.where(row == i, level, column)
+
+    weight = lax.fori_loop(0, kept, pick_weight, jnp.zeros((kept, 1), F32))
+
+    low = iota((count, LANES), 1) < HEAD_DIM
+    arrive(QKV_SUM, qkv_sum)
+    total = summed(qkv_sum)
+    va, vb, vc, vk, vv = (total[:, LANES * i : LANES * (i + 1)] for i in range(5))
+    q0 = jnp.where(low, va, vb).astype(BF16)
+    q1 = jnp.where(low, pltpu.roll(va, HEAD_DIM, 1), pltpu.roll(vc, HEAD_DIM, 1)).astype(BF16)
+    q2 = jnp.where(low, vb, vc).astype(BF16)
+    own_key = vk.astype(BF16)
+    own_value = vv.astype(BF16)
+    qkv_all[b] = jnp.concatenate([q0, q1, q2, own_key, own_value], axis=1)
+    send(QKV_ALL, lambda peer: qkv_all.at[b], qkv_all)
+
+    scale = HEAD_DIM ** (-0.5)
+    same_head = (
+        iota((LANES, LANES), 0) // HEAD_DIM == iota((LANES, LANES), 1) // HEAD_DIM
+    ).astype(F32)
+    own_score = jnp.concatenate(
+        [
+            jnp.dot(
+                q.astype(F32) * own_key.astype(F32),
+                same_head,
+                precision=HIGH,
+                preferred_element_type=F32,
+            )
+            for q in (q0, q1, q2)
+        ],
+        axis=1,
+    ) * scale
+    own_value3 = jnp.concatenate([own_value.astype(F32)] * group, axis=1)
+    heads = group * KV_HEADS
+    rows = count * heads
+    places = count * span
+    place = iota((1, places), 1)
+    limit = jnp.zeros((1, places), jnp.int32)
+    for r in range(count):
+        limit = jnp.where(place // span == r, lengths[0, r], limit)
+    in_cache = b * span + lax.rem(place, span) < limit
+    valid = jnp.logical_and(iota((rows, 1), 0) // heads == place // span, in_cache)
+    head_lanes = (
+        iota((KV_HEADS, kv_width), 1) // HEAD_DIM == iota((KV_HEADS, kv_width), 0)
+    ).astype(F32)[None]
+    loads[1].wait()
+    loads[2].wait()
+
+    arrive(QKV_ALL, qkv_all)
+    for j in range(n):
+        spot = slice(LANES * j, LANES * (j + 1))
+        keys_o[0, :, spot] = qkv_all[j, :, cols : cols + LANES]
+        values_o[0, :, spot] = qkv_all[j, :, cols + LANES : cols + 2 * LANES]
+    spread = []
+    for i in range(group):
+        query = jnp.concatenate(
+            [qkv_all[j, :, LANES * i : LANES * (i + 1)] for j in range(n)], axis=1
+        )
+        spread.append(query.astype(F32)[:, None, :] * head_lanes)
+    spread = jnp.concatenate(spread, axis=1).reshape(rows, kv_width).astype(BF16)
+    scores = (
+        lax.dot_general(
+            spread,
+            key_v[...].reshape(places, kv_width),
+            (((1,), (1,)), ((), ())),
+            preferred_element_type=F32,
+        )
+        * scale
+    )
+    top = jnp.max(jnp.where(valid, scores, -1e30), axis=1, keepdims=True)
+    probs = jnp.exp(jnp.where(valid, scores - top, -1e30))
+    mass = jnp.sum(probs, axis=1, keepdims=True)
+    acc = jnp.dot(
+        probs.astype(BF16), value_v[...].reshape(places, kv_width), preferred_element_type=F32
+    ).reshape(count, heads, kv_width)
+    for i in range(group):
+        mine = jnp.sum(acc[:, KV_HEADS * i : KV_HEADS * (i + 1), :] * head_lanes, axis=1)
+        for j in range(n):
+            att_part[j, :, LANES * i : LANES * (i + 1)] = mine[
+                :, LANES * j : LANES * (j + 1)
+            ].astype(BF16)
+    lane = iota((heads, LANES), 1)
+    slot = iota((heads, LANES), 0)
+    packed = jnp.where(lane[None] == slot[None], top.reshape(count, heads, 1), 0.0) + jnp.where(
+        lane[None] == slot[None] + HEAD_DIM, mass.reshape(count, heads, 1), 0.0
+    )
+    att_stat[b] = jnp.sum(packed, axis=1)
+    att_sum[b] = att_part[b]
+    send(ATT_STAT, lambda peer: att_stat.at[b], att_stat)
+    send(ATT_SUM, lambda peer: att_part.at[peer], att_sum)
+
+    from_lane = iota((LANES, cols), 0)
+    to_lane = iota((LANES, cols), 1)
+    head_of = (
+        to_lane // LANES * KV_HEADS
+        + b * (KV_HEADS // n)
+        + lax.rem(to_lane, LANES) // HEAD_DIM
+    )
+    pick_top = (from_lane == head_of).astype(F32)
+    pick_mass = (from_lane == head_of + HEAD_DIM).astype(F32)
+    loads[3].wait()
+    arrive(ATT_STAT, att_stat)
+    stats = att_stat[...].reshape(n * count, LANES)
+    tops = jnp.dot(stats, pick_top, precision=HIGH, preferred_element_type=F32)
+    masses = jnp.dot(stats, pick_mass, precision=HIGH, preferred_element_type=F32)
+    best = own_score
+    for j in range(n):
+        best = jnp.maximum(best, tops[count * j : count * (j + 1)])
+    own_prob = jnp.exp(own_score - best)
+    denominator = own_prob
+    numerator = own_prob.astype(BF16).astype(F32) * own_value3
+    arrive(ATT_SUM, att_sum)
+    for j in range(n):
+        share = jnp.exp(tops[count * j : count * (j + 1)] - best)
+        denominator = denominator + share * masses[count * j : count * (j + 1)]
+        numerator = numerator + share * att_sum[j].astype(F32)
+    a0, a1, a2 = (
+        (numerator / denominator)[:, LANES * i : LANES * (i + 1)] for i in range(group)
+    )
+    turned = pltpu.roll(a1, HEAD_DIM, 1)
+    attn = jnp.concatenate(
+        [jnp.where(low, a0, turned), jnp.where(low, a2, a0), jnp.where(low, turned, a2)], axis=1
+    ).astype(BF16)
+    for j in range(n):
+        out_part[j] = jnp.dot(
+            attn, out_v[:, cols * j : cols * (j + 1)], preferred_element_type=F32
+        ).astype(BF16)
+    out_sum[b] = out_part[b]
+    send(OUT_SUM, lambda peer: out_part.at[peer], out_sum)
+    arrive(OUT_SUM, out_sum)
+    mixed = hidden[0, :, my_cols].astype(F32) + summed(out_sum)
+    mix_all[b] = mixed.astype(BF16)
+    send(MIX_ALL, lambda peer: mix_all.at[b], mix_all)
+    arrive(MIX_ALL, mix_all)
+
+    expert_in = joined(mix_all)
+    inverse = inverse_rms(expert_in.astype(F32))
+    choice = jnp.dot(expert_in, router[...], preferred_element_type=F32) * inverse
+    expert = iota((count, EXPERTS), 1)
+    is_first = (expert == routes[0, :, 0:1]).astype(F32)
+    is_second = (expert == routes[0, :, 1:2]).astype(F32)
+    gap = jnp.sum((is_first - is_second) * choice, axis=1, keepdims=True)
+    first = 1.0 / (1.0 + jnp.exp(-gap))
+    per_expert = is_first * first + is_second * (1.0 - first)
+
+    def expert_tile(i, out):
+        gate_load(i).wait()
+        gate = jnp.dot(expert_in, gate_v[i], preferred_element_type=F32) * inverse
+        up_load(i).wait()
+        upper = jnp.dot(expert_in, up_v[i], preferred_element_type=F32) * inverse
+        owner = (b * tiles + i) * TILE // EXPERT_UNITS
+        share = jnp.sum(jnp.where(expert == owner, per_expert, 0.0), axis=1, keepdims=True)
+        act = (gate / (1.0 + jnp.exp(-gate)) * upper * share).astype(BF16)
+        down_load(i).wait()
+        return out + jnp.dot(act, down_v[i], preferred_element_type=F32)
+
+    expert_out = lax.fori_loop(0, tiles, expert_tile, jnp.zeros((count, width), F32))
+    for j in range(n):
+        exp_part[j] = expert_out[:, cols * j : cols * (j + 1)].astype(BF16)
+    exp_sum[b] = exp_part[b]
+    send(EXP_SUM, lambda peer: exp_part.at[peer], exp_sum)
+    arrive(EXP_SUM, exp_sum)
+    fin_all[b] = (mixed + summed(exp_sum)).astype(BF16)
+    send(FIN_ALL, lambda peer: fin_all.at[b], fin_all)
+    arrive(FIN_ALL, fin_all)
+    final_own[...] = joined(fin_all)
+
+    def final_copy(to_batch, landing_slot, send_slot):
+        return pltpu.make_async_remote_copy(
+            src_ref=final_own,
+            dst_ref=final_all.at[landing_slot],
+            send_sem=fin_send.at[send_slot],
+            recv_sem=fin_recv.at[landing_slot],
+            device_id={"guide": t // half, "batch": to_batch},
+            device_id_type=MESH,
+        )
+
+    my_slot = g * half + lax.rem(t, half)
+    stays = g == t // half
+    for k in range(1, nb):
+        final_copy(lax.rem(t + k, nb), my_slot, k).start()
+
+    @pl.when(stays)
+    def _():
+        final_all[my_slot] = final_own[...]
+
+    @pl.when(jnp.logical_not(stays))
+    def _():
+        final_copy(t, my_slot, 0).start()
+
+    for s in range(2):
+        for j in range(half):
+            from_me = jnp.logical_and(g == s, t == g * half + j)
+
+            @pl.when(jnp.logical_not(from_me))
+            def _():
+                final_copy(t, s * half + j, 0).wait_recv()
+
+    finals = final_all[...].reshape(2 * half * count, width)
+    inverse = inverse_rms(finals.astype(F32))
+
+    def vocab_tile(i, carry):
+        vocab_load(i).wait()
+        streams = jnp.dot(finals, vocab_v[i], preferred_element_type=F32) * inverse
+        cond, uncond = streams[:kept], streams[kept:]
+        logits_o[:, tile_cols(i)] = uncond + weight * (cond - uncond)
+        return carry
+
+    lax.fori_loop(0, vocab_tiles, vocab_tile, 0)
+
+    for phase, landing in (
+        (QKV_SUM, qkv_sum),
+        (QKV_ALL, qkv_all),
+        (ATT_SUM, att_sum),
+        (ATT_STAT, att_stat),
+        (OUT_SUM, out_sum),
+        (MIX_ALL, mix_all),
+        (EXP_SUM, exp_sum),
+        (FIN_ALL, fin_all),
+    ):
+        drain(phase, landing)
+    for k in range(1, nb):
+        final_copy(lax.rem(t + k, nb), my_slot, k).wait_send()
+
+    @pl.when(jnp.logical_not(stays))
+    def _():
+        final_copy(t, my_slot, 0).wait_send()
+
+
+def local_kernel(
+    n,
+    nb,
+    hidden,
+    w_qkv,
+    key_cache,
+    value_cache,
+    lengths,
+    w_out,
+    router,
+    routes,
+    w_gate,
+    w_up,
+    w_down,
+    w_vocab,
+    group_ids,
+    weight_index,
+    guidance_levels,
+):
+    count, width = hidden.shape[1:]
+    span, kv_width = key_cache.shape[2:]
+    cols = width // n
+    units = w_gate.shape[1]
+    vocab = w_vocab.shape[1]
+    half = nb // 2
+    kept = half * count
+    vmem = pl.BlockSpec(memory_space=pltpu.VMEM)
+    smem = pl.BlockSpec(memory_space=pltpu.SMEM)
+    anywhere = pl.BlockSpec(memory_space=pl.ANY)
+    packed = cols + 2 * LANES
+    chunk = pltpu.VMEM((n, count, cols), BF16)
+    tiles, vocab_tiles = units // TILE, vocab // TILE
+    weights = 2 * (3 * width * units + width * vocab + w_qkv.size + w_out.size)
+    return pl.pallas_call(
+        functools.partial(step_kernel, n, nb),
+        out_shape=(
+            jax.ShapeDtypeStruct((kept, vocab), F32),
+            jax.ShapeDtypeStruct((1, count, kv_width), BF16),
+            jax.ShapeDtypeStruct((1, count, kv_width), BF16),
+        ),
+        in_specs=[vmem, smem, vmem, vmem, smem, smem, smem] + [anywhere] * 8,
+        out_specs=(vmem, vmem, vmem),
+        scratch_shapes=[
+            pltpu.VMEM(w_qkv.shape, BF16),
+            pltpu.VMEM(key_cache.shape[1:], BF16),
+            pltpu.VMEM(value_cache.shape[1:], BF16),
+            pltpu.VMEM(w_out.shape, BF16),
+            pltpu.VMEM((tiles, width, TILE), BF16),
+            pltpu.VMEM((tiles, width, TILE), BF16),
+            pltpu.VMEM((tiles, TILE, width), BF16),
+            pltpu.VMEM((vocab_tiles, width, TILE), BF16),
+            pltpu.VMEM((n, count, packed), F32),
+            pltpu.VMEM((n, count, packed), F32),
+            pltpu.VMEM((n, count, packed), BF16),
+            chunk,
+            chunk,
+            pltpu.VMEM((n, count, LANES), F32),
+            chunk,
+            chunk,
+            chunk,
+            chunk,
+            chunk,
+            chunk,
+            pltpu.VMEM((count, width), BF16),
+            pltpu.VMEM((2 * half, count, width), BF16),
+            pltpu.SemaphoreType.DMA((4,)),
+            pltpu.SemaphoreType.DMA((4, max(tiles, vocab_tiles))),
+            pltpu.SemaphoreType.DMA((PHASES, n)),
+            pltpu.SemaphoreType.DMA((PHASES, n)),
+            pltpu.SemaphoreType.DMA((nb,)),
+            pltpu.SemaphoreType.DMA((2 * half,)),
+        ],
+        compiler_params=pltpu.CompilerParams(
+            collective_id=0, has_side_effects=True, vmem_limit_bytes=60 * 2**20
+        ),
+        cost_estimate=pl.CostEstimate(
+            flops=weights * count, bytes_accessed=weights, transcendentals=count * units
+        ),
+    )(
+        hidden,
+        lengths,
+        router,
+        routes,
+        group_ids,
+        weight_index,
+        guidance_levels,
+        w_qkv,
+        key_cache,
+        value_cache,
+        w_out,
+        w_gate,
+        w_up,
+        w_down,
+        w_vocab,
+    )
+
+
+def fits_kernel(mesh):
+    return KV_HEADS * HEAD_DIM == mesh.shape["blk"] * LANES and mesh.shape["batch"] % 2 == 0
+
+
 def solution(mesh):
+    if fits_kernel(mesh):
+        body = functools.partial(local_kernel, mesh.shape["blk"], mesh.shape["batch"])
+    else:
+        body = local
     placed = (
         P("guide", "batch", None),
         P("blk", None),
@@ -156,7 +692,7 @@
         P(),
     )
     return jax.shard_map(
-        local,
+        body,
         mesh=mesh,
         in_specs=placed,
         out_specs=(

time: 210 us -> 60.6 us (0.29)
  waiting for transfers between devices: 83.8 us -> 0 us
  blocking collectives: 67.4 us -> 0 us
  Pallas kernels: 0 us -> 52 us
  matrix products: 29.2 us -> 0 us
  between operations: 14 us -> 0.64 us
  other arithmetic: 10.2 us -> 0 us
  local copies, waits for them, and re-layouts: 4.36 us -> 7.59 us
    psum x3 -> x0, waiting for transfers between devices: 82.6 us -> none  [the longest x1 34.7 us: local(): lax.psum(jnp.dot(attn_cols, w_out, preferred_element_type=jnp.float32), '...]
    pallas_call x0 -> x1, Pallas kernels: none -> 52 us  [local_kernel(): pl.pallas_call(functools.partial(step_kernel, n, nb), out_shape=(jax.Shap...]
    psum x2 -> x0, blocking collectives: 42.4 us -> none  [the longest x1 23.6 us: local(): qkv = lax.psum(partial_qkv, 'blk').astype(jnp.bfloat16)]
    dot_general x9 -> x0, matrix products: 29.2 us -> none  [the longest x1 12.2 us: local(): jnp.dot(act, w_down, preferred_element_type=jnp.float32)]
    pmax x1 -> x0, blocking collectives: 16.3 us -> none  [local(): top = lax.pmax(jnp.maximum(local_top, own), 'blk')]
    all_gather x1 -> x0, blocking collectives: 8.65 us -> none  [local(): lax.all_gather(final_in, 'batch', axis=0, tiled=True)]
    unnamed x16 -> x5, local copies, waits for them, and re-layouts: 0.04 us -> 7.59 us
    reduce_sum x9 -> x0, other arithmetic: 4.68 us -> none  [the longest x3 2.96 us: rms(): jnp.mean(values * values, axis=-1, keepdims=True) + EPS]
  transfers between devices with their start and end apart: 4 -> 0, of which waited for: 4 -> 0; matrix products, arithmetic and copies ran while one was open for 1% -> 0% of each run, Pallas kernels for 0% -> 0%
where the time goes in v1:
time: 60.6 us; the launch traced here: 60.2 us
  Pallas kernels  52 us (86%)
  local copies, waits for them, and re-layouts  7.59 us (13%)
  between operations  0.64 us (1%)
    pallas_call x1, Pallas kernels, local_kernel(): pl.pallas_call(functools.partial(step_kernel, n, nb), out_shape=(jax.Shap...  52 us
    unnamed x5, local copies, waits for them, and re-layouts  7.59 us

profile of v1, /device:TPU:0, one launch (start us, length us, event | category | flops | bytes accessed | tf_op | source)
XLA Modules:
  0.0 60.2 jit_solution(11305738659685597731)
XLA Ops:
  0.6 1.4 %copy.19.routes = s32[1,16,2]{2,1,0:T(8,128)} copy(s32[1,16,2]{1,2,0:T(2,128)} %param.22) | data formatting | bytes 256 | tf_op args[7]
  2.0 1.7 %copy.18.router = bf16[1536,16]{1,0:T(8,128)(2,1)} copy(bf16[1536,16]{0,1:T(8,128)(2,1)} %param.21) | data formatting | bytes 98304 | tf_op args[6]
  3.7 52.0 %shard_map.166 = (f32[32,4096]{1,0:T(8,128)}, bf16[1,16,512]{2,1,0:T(8,128)(2,1)}, bf16[1,16,512]{2,1,0:T(8,128)(2,1)}) custom-call(bf16[1,16,1536]{2,1,0:T(8,128)(2,1)} %hidden.1, s32[1,16]{1,0:T(1,128)} %lengths.1, bf16[1536,16]{1,0:T(8,128)(2,1)} %copy.18.router, s32[1,16,2]{2,1,0:T(8,128)} %copy.19.routes, s32[64]{0:T(128)} %group_ids.1, s32[8]{0:T(128)} %weight_index.1, ...), custom_call_target="tpu_custom_call" | custom-call | flops 855638016 | bytes 53477376 | tf_op jit(solution)/shard_map/pallas_call | solution.py:604
  55.7 1.9 %copy.23 = f32[32,4096]{1,0:T(8,128)} copy(f32[32,4096]{1,0:T(8,128)} %get-tuple-element.6) | data formatting | bytes 1048576
  57.6 1.3 %copy.24 = bf16[1,16,512]{2,1,0:T(8,128)(2,1)} copy(bf16[1,16,512]{2,1,0:T(8,128)(2,1)} %get-tuple-element.7) | data formatting | bytes 32768
  58.9 1.3 %copy.25 = bf16[1,16,512]{2,1,0:T(8,128)(2,1)} copy(bf16[1,16,512]{2,1,0:T(8,128)(2,1)} %get-tuple-element.8) | data formatting | bytes 32768

commit v2 on v1

--- a/solution.py
+++ b/solution.py
@@ -343,6 +343,13 @@
 
     weight = lax.fori_loop(0, kept, pick_weight, jnp.zeros((kept, 1), F32))
 
+    request = iota((count, 1), 0)
+    chosen_first = jnp.zeros((count, 1), jnp.int32)
+    chosen_second = jnp.zeros((count, 1), jnp.int32)
+    for r in range(count):
+        chosen_first = jnp.where(request == r, routes[0, 0, r], chosen_first)
+        chosen_second = jnp.where(request == r, routes[0, 1, r], chosen_second)
+
     low = iota((count, LANES), 1) < HEAD_DIM
     arrive(QKV_SUM, qkv_sum)
     total = summed(qkv_sum)
@@ -476,10 +483,15 @@
 
     expert_in = joined(mix_all)
     inverse = inverse_rms(expert_in.astype(F32))
-    choice = jnp.dot(expert_in, router[...], preferred_element_type=F32) * inverse
+    choice = (
+        lax.dot_general(
+            expert_in, router[...], (((1,), (1,)), ((), ())), preferred_element_type=F32
+        )
+        * inverse
+    )
     expert = iota((count, EXPERTS), 1)
-    is_first = (expert == routes[0, :, 0:1]).astype(F32)
-    is_second = (expert == routes[0, :, 1:2]).astype(F32)
+    is_first = (expert == chosen_first).astype(F32)
+    is_second = (expert == chosen_second).astype(F32)
     gap = jnp.sum((is_first - is_second) * choice, axis=1, keepdims=True)
     first = 1.0 / (1.0 + jnp.exp(-gap))
     per_expert = is_first * first + is_second * (1.0 - first)
@@ -566,6 +578,19 @@
     @pl.when(jnp.logical_not(stays))
     def _():
         final_copy(t, my_slot, 0).wait_send()
+
+
+def write_kernel(logits, keys, values, logits_o, keys_o, values_o, sem):
+    copies = [
+        pltpu.make_async_copy(source, target, sem.at[i])
+        for i, (source, target) in enumerate(
+            ((logits, logits_o), (keys, keys_o), (values, values_o))
+        )
+    ]
+    for copy in copies:
+        copy.start()
+    for copy in copies:
+        copy.wait()
 
 
 def local_kernel(
@@ -597,18 +622,19 @@
     vmem = pl.BlockSpec(memory_space=pltpu.VMEM)
     smem = pl.BlockSpec(memory_space=pltpu.SMEM)
     anywhere = pl.BlockSpec(memory_space=pl.ANY)
+    in_hbm = pl.BlockSpec(memory_space=pltpu.HBM)
     packed = cols + 2 * LANES
     chunk = pltpu.VMEM((n, count, cols), BF16)
     tiles, vocab_tiles = units // TILE, vocab // TILE
     weights = 2 * (3 * width * units + width * vocab + w_qkv.size + w_out.size)
-    return pl.pallas_call(
+    results = pl.pallas_call(
         functools.partial(step_kernel, n, nb),
         out_shape=(
             jax.ShapeDtypeStruct((kept, vocab), F32),
             jax.ShapeDtypeStruct((1, count, kv_width), BF16),
             jax.ShapeDtypeStruct((1, count, kv_width), BF16),
         ),
-        in_specs=[vmem, smem, vmem, vmem, smem, smem, smem] + [anywhere] * 8,
+        in_specs=[vmem, smem, vmem, smem, smem, smem, smem] + [anywhere] * 8,
         out_specs=(vmem, vmem, vmem),
         scratch_shapes=[
             pltpu.VMEM(w_qkv.shape, BF16),
@@ -649,8 +675,8 @@
     )(
         hidden,
         lengths,
-        router,
-        routes,
+        router.T,
+        jnp.swapaxes(routes, 1, 2),
         group_ids,
         weight_index,
         guidance_levels,
@@ -663,6 +689,14 @@
         w_down,
         w_vocab,
     )
+    return pl.pallas_call(
+        write_kernel,
+        out_shape=tuple(jax.ShapeDtypeStruct(part.shape, part.dtype) for part in results),
+        in_specs=[in_hbm] * 3,
+        out_specs=(in_hbm,) * 3,
+        scratch_shapes=[pltpu.SemaphoreType.DMA((3,))],
+        compiler_params=pltpu.CompilerParams(vmem_limit_bytes=60 * 2**20),
+    )(*results)
 
 
 def fits_kernel(mesh):

time: 60.6 us -> 70.7 us (1.17)
  Pallas kernels: 52 us -> 69.8 us
  local copies, waits for them, and re-layouts: 7.59 us -> 0 us
    pallas_call x0 -> x1, Pallas kernels: none -> 18 us  [local_kernel(): pl.pallas_call(write_kernel, out_shape=tuple((jax.ShapeDtypeStruct(part.s...]
    unnamed x5 -> x0, local copies, waits for them, and re-layouts: 7.59 us -> none
where the time goes in v2:
time: 70.7 us; the launch traced here: 70.5 us
  Pallas kernels  69.8 us (99%)
    pallas_call x1, Pallas kernels, local_kernel(): pl.pallas_call(functools.partial(step_kernel, n, nb), out_shape=(jax.Shap...  51.8 us
    pallas_call x1, Pallas kernels, local_kernel(): pl.pallas_call(write_kernel, out_shape=tuple((jax.ShapeDtypeStruct(part.s...  18 us

profile of v2, /device:TPU:0, one launch (start us, length us, event | category | flops | bytes accessed | tf_op | source)
XLA Modules:
  0.0 70.5 jit_solution(17676944677875900413)
XLA Ops:
  0.6 51.8 %shard_map.166 = (f32[32,4096]{1,0:T(8,128)}, bf16[1,16,512]{2,1,0:T(8,128)(2,1)}, bf16[1,16,512]{2,1,0:T(8,128)(2,1)}) custom-call(bf16[1,16,1536]{2,1,0:T(8,128)(2,1)} %hidden.1, s32[1,16]{1,0:T(1,128)} %lengths.1, bf16[16,1536]{1,0:T(8,128)(2,1)} %bitcast.2, s32[1,2,16]{2,1,0:T(2,128)} %bitcast.3, s32[64]{0:T(128)} %group_ids.1, s32[8]{0:T(128)} %weight_index.1, ...), custom_call_target="tpu_custom_call" | custom-call | flops 855638016 | bytes 53477376 | tf_op jit(solution)/shard_map/pallas_call | solution.py:630
  52.5 18.0 %shard_map.167 = (f32[32,4096]{1,0:T(8,128)}, bf16[1,16,512]{2,1,0:T(8,128)(2,1)}, bf16[1,16,512]{2,1,0:T(8,128)(2,1)}) custom-call(f32[32,4096]{1,0:T(8,128)} %get-tuple-element.6.logits, bf16[1,16,512]{2,1,0:T(8,128)(2,1)} %get-tuple-element.7.keys, bf16[1,16,512]{2,1,0:T(8,128)(2,1)} %get-tuple-element.8.values), custom_call_target="tpu_custom_call" | custom-call | tf_op jit(solution)/shard_map/pallas_call | solution.py:692

commit v3 on v2

--- a/solution.py
+++ b/solution.py
@@ -580,17 +580,10 @@
         final_copy(t, my_slot, 0).wait_send()
 
 
-def write_kernel(logits, keys, values, logits_o, keys_o, values_o, sem):
-    copies = [
-        pltpu.make_async_copy(source, target, sem.at[i])
-        for i, (source, target) in enumerate(
-            ((logits, logits_o), (keys, keys_o), (values, values_o))
-        )
-    ]
-    for copy in copies:
-        copy.start()
-    for copy in copies:
-        copy.wait()
+def write_kernel(logits, keys, values, logits_o, keys_o, values_o):
+    logits_o[...] = logits[...]
+    keys_o[...] = keys[...]
+    values_o[...] = values[...]
 
 
 def local_kernel(
@@ -622,7 +615,6 @@
     vmem = pl.BlockSpec(memory_space=pltpu.VMEM)
     smem = pl.BlockSpec(memory_space=pltpu.SMEM)
     anywhere = pl.BlockSpec(memory_space=pl.ANY)
-    in_hbm = pl.BlockSpec(memory_space=pltpu.HBM)
     packed = cols + 2 * LANES
     chunk = pltpu.VMEM((n, count, cols), BF16)
     tiles, vocab_tiles = units // TILE, vocab // TILE
@@ -692,10 +684,8 @@
     return pl.pallas_call(
         write_kernel,
         out_shape=tuple(jax.ShapeDtypeStruct(part.shape, part.dtype) for part in results),
-        in_specs=[in_hbm] * 3,
-        out_specs=(in_hbm,) * 3,
-        scratch_shapes=[pltpu.SemaphoreType.DMA((3,))],
-        compiler_params=pltpu.CompilerParams(vmem_limit_bytes=60 * 2**20),
+        in_specs=[vmem] * 3,
+        out_specs=(vmem,) * 3,
     )(*results)
 
 

time: 70.7 us -> 54.6 us (0.77)
  Pallas kernels: 69.8 us -> 53.7 us
    pallas_call x1, Pallas kernels: 18 us -> 1.89 us  [local_kernel(): pl.pallas_call(write_kernel, out_shape=tuple((jax.ShapeDtypeStruct(part.s...]
where the time goes in v3:
time: 54.6 us; the launch traced here: 54.4 us
  Pallas kernels  53.7 us (98%)
  between operations  0.64 us (1%)
    pallas_call x1, Pallas kernels, local_kernel(): pl.pallas_call(functools.partial(step_kernel, n, nb), out_shape=(jax.Shap...  51.8 us
    pallas_call x1, Pallas kernels, local_kernel(): pl.pallas_call(write_kernel, out_shape=tuple((jax.ShapeDtypeStruct(part.s...  1.89 us

profile of v3, /device:TPU:0, one launch (start us, length us, event | category | flops | bytes accessed | tf_op | source)
XLA Modules:
  0.0 54.4 jit_solution(12743071104053137207)
XLA Ops:
  0.6 51.8 %shard_map.166 = (f32[32,4096]{1,0:T(8,128)}, bf16[1,16,512]{2,1,0:T(8,128)(2,1)}, bf16[1,16,512]{2,1,0:T(8,128)(2,1)}) custom-call(bf16[1,16,1536]{2,1,0:T(8,128)(2,1)} %hidden.1, s32[1,16]{1,0:T(1,128)} %lengths.1, bf16[16,1536]{1,0:T(8,128)(2,1)} %bitcast.2, s32[1,2,16]{2,1,0:T(2,128)} %bitcast.3, s32[64]{0:T(128)} %group_ids.1, s32[8]{0:T(128)} %weight_index.1, ...), custom_call_target="tpu_custom_call" | custom-call | flops 855638016 | bytes 53477376 | tf_op jit(solution)/shard_map/pallas_call | solution.py:622
  52.5 1.9 %shard_map.167 = (f32[32,4096]{1,0:T(8,128)}, bf16[1,16,512]{2,1,0:T(8,128)(2,1)}, bf16[1,16,512]{2,1,0:T(8,128)(2,1)}) custom-call(f32[32,4096]{1,0:T(8,128)} %get-tuple-element.6.logits, bf16[1,16,512]{2,1,0:T(8,128)(2,1)} %get-tuple-element.7.keys, bf16[1,16,512]{2,1,0:T(8,128)(2,1)} %get-tuple-element.8.values), custom_call_target="tpu_custom_call" | custom-call | tf_op jit(solution)/shard_map/pallas_call | solution.py:684
